TPU v7x, 32 devices: a whole 2x2x4 slice. The times are simulated.
32 devices in a mesh: job: 2 (over y), fsdp: 8 (over z, x), tp: 2 (over core).
Axes of the slice: x: 2, y: 2, z: 4, core: 2. Of those that a mesh axis runs over, the one named last changes fastest.
Arguments:
- weight: bfloat16 [8192, 16384], P(('job', 'fsdp'), 'tp'), parts along dimension 0, may hold values from -0.09375 to 0.09375
- grad: bfloat16 [8192, 16384], P(('job', 'fsdp'), 'tp'), parts along dimension 0, may hold values from -36 to 36
- row_moment: float32 [8192], P(('job', 'fsdp')), parts along dimension 0, may hold values from 0.01 to 10
- col_moment: float32 [32768], P(('job', 'tp')), parts along dimension 0, may hold values from 0.01 to 10
- states: bfloat16 [768, 4096], P(('job', 'fsdp')), parts along dimension 0, may hold values from -6 to 6
- norm_gain: bfloat16 [8192], P('job'), parts along dimension 0, may hold values from 0.099609375 to 1.8984375
- gate_values: bfloat16 [768, 16384], P(('job', 'fsdp'), 'tp'), parts along dimension 0, may hold values from -8 to 8
Outputs:
- new_weight: bfloat16 [8192, 16384], P(('job', 'fsdp'), 'tp'), parts along dimension 0
- new_rows: float32 [8192], P(('job', 'fsdp')), parts along dimension 0
- new_columns: float32 [32768], P(('job', 'tp')), parts along dimension 0
- hidden: bfloat16 [768, 16384], P(('job', 'fsdp'), 'tp'), parts along dimension 0
There are 2 independent parts, one for each index of `job`. A program takes and returns all parts, laid end to end along the dimension named above; each array names one. Nothing has to cross between parts.
All inputs are finite; a program needn't handle non-finite values.
Results may differ from a plain program's by a relative error of at most 0.002.
The roundings to bfloat16 on the way count: a program that leaves them out, or rounds other values in their place, can miss the bound.
Values may be sent and summed in bfloat16 or wider, within the bound.
A program may use at most 128 MiB of HBM per device.

v0:
```python
import jax
import jax.numpy as jnp
from jax import lax
from jax.sharding import PartitionSpec as P

D = 4096
FF = 16384


def on_device(weight, grad, row_moment, col_moment, states, norm_gain, gate_values):
    gradient = grad.astype(jnp.float32)
    squares = gradient * gradient + 1e-30
    row_partial = jnp.sum(squares, axis=1)
    col_partial = jnp.sum(squares, axis=0)
    row_total = lax.psum(row_partial, "tp")
    new_rows = 0.8 * row_moment + 0.2 * (row_total / FF)
    col_total, rows_summed = lax.psum((col_partial, jnp.sum(new_rows)), "fsdp")
    new_columns = 0.8 * col_moment + 0.2 * (col_total / D)
    row_scale = rows_summed / D
    update = gradient / jnp.sqrt(new_rows[:, None] * new_columns[None, :] / row_scale)
    new_weight = (weight.astype(jnp.float32) - 0.01 * update).astype(jnp.bfloat16)
    values = states.astype(jnp.float32)
    normed = (
        values
        * lax.rsqrt(jnp.mean(values * values, axis=1, keepdims=True) + 1e-06)
        * norm_gain.astype(jnp.float32)
    ).astype(jnp.bfloat16)
    column_block = lax.all_to_all(new_weight, "fsdp", split_axis=1, concat_axis=0, tiled=True)
    up_block = jnp.dot(
        lax.all_gather(normed, "fsdp", axis=0, tiled=True),
        column_block,
        preferred_element_type=jnp.float32,
    ).astype(jnp.bfloat16)
    up_values = lax.all_to_all(up_block, "fsdp", split_axis=0, concat_axis=1, tiled=True)
    hidden = (jax.nn.silu(gate_values.astype(jnp.float32)) * up_values.astype(jnp.float32)).astype(
        jnp.bfloat16
    )
    return (new_weight, new_rows, new_columns, hidden)


def solution(mesh):
    return jax.shard_map(
        on_device,
        mesh=mesh,
        in_specs=(
            P(("job", "fsdp"), "tp"),
            P(("job", "fsdp"), "tp"),
            P(("job", "fsdp")),
            P(("job", "tp")),
            P(("job", "fsdp"), None),
            P("job"),
            P(("job", "fsdp"), "tp"),
        ),
        out_specs=(
            P(("job", "fsdp"), "tp"),
            P(("job", "fsdp")),
            P(("job", "tp")),
            P(("job", "fsdp"), "tp"),
        ),
        check_vma=False,
    )
```

profile of v0, /device:TPU:0, one launch (start us, length us, event | category | flops | bytes accessed | tf_op | source)
XLA Modules:
  0.0 364.7 jit_solution(2425789617691000187)
XLA Ops:
  7.2 11.9 %copy.14 = bf16[512,8192]{0,1:T(8,128)(2,1)} copy(bf16[512,8192]{1,0:T(8,128)(2,1)} %param.8) | data formatting | bytes 16777216 | tf_op args[1]
  19.1 6.7 %fusion.1 = (f32[8192]{0:T(1024)S(1)}, f32[512]{0:T(512)S(1)}) fusion(bf16[512,8192]{0,1:T(8,128)(2,1)} %copy.14), kind=kLoop, calls=%fused_computation.3 | loop fusion | flops 20962816 | bytes 8423424 | tf_op jit(solution)/shard_map/reduce_sum | solution.py:14
  25.8 2.6 psum.21
  28.4 0.0 copy-start.6
  28.4 0.0 copy-start.3
  28.4 11.9 %copy.13 = bf16[512,8192]{0,1:T(8,128)(2,1)} copy(bf16[512,8192]{1,0:T(8,128)(2,1)} %param.7) | data formatting | bytes 16777216 | tf_op args[0]
  40.4 0.0 copy-done.6
  40.4 0.6 fusion.14
  41.0 0.0 copy-start.4
  41.0 40.2 %all-reduce = (f32[]{:T(128)}, f32[8192]{0:T(1024)S(1)}) all-reduce(f32[]{:T(128)} %get-tuple-element.12, f32[8192]{0:T(1024)S(1)} %get-tuple-element.8), channel_id=1, replica_groups=mesh['job'=2,'fsdp'=8,'tp'=2] {'fsdp'}, use_global_device_ids=true, to_apply=%region_5.0 | all-reduce | flops 8193 | bytes 65544 | tf_op jit(solution)/shard_map/psum | solution.py:17
  81.1 0.0 copy-done.3
  81.2 0.0 copy-start.2
  81.8 11.0 %fusion.5 = bf16[512,8192]{0,1:T(8,128)(2,1)} fusion(bf16[512,8192]{0,1:T(8,128)(2,1)} %copy.14, bf16[512,8192]{0,1:T(8,128)(2,1)} %copy.13, f32[]{:T(128)S(6)} %div.26, f32[8192]{0:T(1024)S(1)} %multiply_add_fusion, f32[512]{0:T(512)S(1)} %get-tuple-element.13), kind=kLoop, calls=%fused_computation.7 | loop fusion | flops 33554432 | bytes 25200644 | tf_op jit(solution)/shard_map/convert_element_type | solution.py:21
  92.9 0.0 copy-done.4
  92.9 0.0 copy-done.2
  92.9 0.0 copy-start.5
  92.9 0.0 copy-start
  92.9 5.1 %all-to-all-start = ((bf16[512,8,1024]{0,2,1:T(8,128)(2,1)}), bf16[512,8,1024]{0,2,1:T(8,128)(2,1)}, u32[]{:S(2)}, u32[]{:S(2)}) async-start(bf16[512,8,1024]{0,2,1:T(8,128)(2,1)} %bitcast.10), calls=%async_computation | async-start | bytes 16777216 | tf_op jit(solution)/shard_map/all_to_all | solution.py:28
  98.0 0.0 all-gather.2.cloned.1.call-start
  98.1 0.0 copy-done.5
  98.1 0.0 copy-done
  98.1 0.2 fusion.11
  98.3 0.9 fusion.13
  99.2 0.0 all-gather.2.cloned.1.call-update
  99.2 213.1 %all-to-all-done = bf16[512,8,1024]{0,2,1:T(8,128)(2,1)} async-done(((bf16[512,8,1024]{0,2,1:T(8,128)(2,1)}), bf16[512,8,1024]{0,2,1:T(8,128)(2,1)}, u32[]{:S(2)}, u32[]{:S(2)}) %all-to-all-start) | async-done | bytes 8388640 | tf_op jit(solution)/shard_map/all_to_all | solution.py:28
  312.4 11.4 %copy.15 = bf16[8,512,1024]{2,1,0:T(8,128)(2,1)} copy(bf16[8,512,1024]{1,2,0:T(8,128)(2,1)} %bitcast.1) | data formatting | bytes 16777216 | tf_op jit(solution)/shard_map/all_to_all | solution.py:28
  323.7 0.0 all-gather.2.cloned.1.call-done
  323.7 8.6 %convolution_convert_fusion = bf16[384,1024]{1,0:T(8,128)(2,1)} fusion(bf16[384,4096]{1,0:T(8,128)(2,1)} %all-gather.2.cloned.1.call-done, bf16[4096,1024]{1,0:T(8,128)(2,1)} %bitcast.11), kind=kOutput, calls=%fused_computation.16 | convolution fusion | flops 3221618688 | bytes 12320768 | tf_op jit(solution)/shard_map/dot_general | solution.py:29
  332.3 3.6 all-to-all-start.1
  335.9 0.0 copy-start.1
  335.9 12.0 %copy.17 = bf16[512,8192]{1,0:T(8,128)(2,1)} copy(bf16[512,8192]{0,1:T(8,128)(2,1)} %fusion.5) | data formatting | bytes 16777216
  347.9 8.4 %all-to-all-done.1 = bf16[8,48,1024]{2,1,0:T(8,128)(2,1)S(1)} async-done(((bf16[8,48,1024]{2,1,0:T(8,128)(2,1)}), bf16[8,48,1024]{2,1,0:T(8,128)(2,1)S(1)}, u32[]{:S(2)}, u32[]{:S(2)}) %all-to-all-start.1) | async-done | bytes 786464 | tf_op jit(solution)/shard_map/all_to_all | solution.py:34
  356.3 0.2 convert_bitcast_fusion
  356.5 0.1 copy.18
  356.6 0.0 copy-done.1
  356.6 1.3 fusion.10
  (3 shorter events, 0.0 us)
Async XLA Ops:
  28.4 11.9 %copy-start.6 = (f32[512]{0:T(512)S(1)}, f32[512]{0:T(512)}, u32[]{:S(2)}) copy-start(f32[512]{0:T(512)} %param.9) | copy-start | bytes 6148
  28.4 52.7 %copy-start.3 = (f32[8192]{0:T(1024)S(1)}, f32[8192]{0:T(1024)}, u32[]{:S(2)}) copy-start(f32[8192]{0:T(1024)} %param.10) | copy-start | bytes 98308
  41.0 51.9 %copy-start.4 = (f32[512]{0:T(512)}, f32[512]{0:T(512)S(1)}, u32[]{:S(2)}) copy-start(f32[512]{0:T(512)S(1)} %get-tuple-element.13) | copy-start | bytes 6148
  81.2 11.7 %copy-start.2 = (f32[8192]{0:T(1024)}, f32[8192]{0:T(1024)S(1)}, u32[]{:S(2)}) copy-start(f32[8192]{0:T(1024)S(1)} %multiply_add_fusion) | copy-start | bytes 98308
  92.9 5.2 %copy-start.5 = (bf16[4096]{0:T(1024)(128)(2,1)S(1)}, bf16[4096]{0:T(1024)(128)(2,1)}, u32[]{:S(2)}) copy-start(bf16[4096]{0:T(1024)(128)(2,1)} %param.12) | copy-start | bytes 24580
  92.9 5.2 %copy-start = (bf16[48,4096]{1,0:T(8,128)(2,1)S(1)}, bf16[48,4096]{1,0:T(8,128)(2,1)}, u32[]{:S(2)}) copy-start(bf16[48,4096]{1,0:T(8,128)(2,1)} %param.11) | copy-start | bytes 1179652
  92.9 219.5 %all-to-all-start = ((bf16[512,8,1024]{0,2,1:T(8,128)(2,1)}), bf16[512,8,1024]{0,2,1:T(8,128)(2,1)}, u32[]{:S(2)}, u32[]{:S(2)}) async-start(bf16[512,8,1024]{0,2,1:T(8,128)(2,1)} %bitcast.10), calls=%async_computation | async-start | bytes 16777216 | tf_op jit(solution)/shard_map/all_to_all | solution.py:28
  98.0 225.7 %all-gather.2.cloned.1.call-start = ((), (), s32[]{:S(2)}) async-start(), calls=%async_computation.2 | async-start | bytes 3538944 | tf_op jit(solution)/shard_map/all_gather | solution.py:30
  332.3 24.0 %all-to-all-start.1 = ((bf16[8,48,1024]{2,1,0:T(8,128)(2,1)}), bf16[8,48,1024]{2,1,0:T(8,128)(2,1)S(1)}, u32[]{:S(2)}, u32[]{:S(2)}) async-start(bf16[8,48,1024]{2,1,0:T(8,128)(2,1)} %bitcast.3), calls=%async_computation.1 | async-start | bytes 1572864 | tf_op jit(solution)/shard_map/all_to_all | solution.py:34
  335.9 20.7 %copy-start.1 = (bf16[48,8192]{1,0:T(8,128)(2,1)S(1)}, bf16[48,8192]{1,0:T(8,128)(2,1)}, u32[]{:S(2)}) copy-start(bf16[48,8192]{1,0:T(8,128)(2,1)} %param.13) | copy-start | bytes 2359300
Sparse Core Ops, SparseCore 0:
  101.6 179.9 all-gather.1
where the time goes:
time: 366 us; the launch traced here: 365 us
  waiting for transfers between devices  222 us (61%)
  local copies, waits for them, and re-layouts  47.4 us (13%)
  blocking collectives  42.7 us (12%)
  other arithmetic  21 us (6%)
  between operations  14.8 us (4%)
  starting transfers between devices  8.72 us (2%)
  matrix products  8.63 us (2%)
    all_to_all x1, waiting for transfers between devices, on_device(): lax.all_to_all(new_weight, 'fsdp', split_axis=1, concat_axis=0, tiled=True)  213 us
    psum x1, blocking collectives, on_device(): col_total, rows_summed = lax.psum((col_partial, jnp.sum(new_rows)), 'fsdp')  40.2 us
    unnamed x17, local copies, waits for them, and re-layouts  35.9 us
    all_to_all x1, local copies, waits for them, and re-layouts, on_device(): lax.all_to_all(new_weight, 'fsdp', split_axis=1, concat_axis=0, tiled=True)  11.4 us
    convert_element_type x1, other arithmetic, on_device(): (weight.astype(jnp.float32) - 0.01 * update).astype(jnp.bfloat16)  11 us
    dot_general x1, matrix products, on_device(): jnp.dot(lax.all_gather(normed, 'fsdp', axis=0, tiled=True), column_block,...  8.63 us
    all_to_all x1, waiting for transfers between devices, on_device(): lax.all_to_all(up_block, 'fsdp', split_axis=0, concat_axis=1, tiled=True)  8.39 us
  transfers between devices with their start and end apart: 3, of which 2 were waited for; matrix products, arithmetic and copies ran while one was open for 7% of the time, Pallas kernels for 0%

commit v1 on v0

v1 whole, which is shorter than its diff:
```python
import functools
import jax
import jax.numpy as jnp
from jax import lax
from jax.experimental import pallas as pl
from jax.experimental.pallas import tpu as pltpu
from jax.sharding import PartitionSpec as P

MESH = pl.DeviceIdType.MESH
F32 = jnp.float32
BF16 = jnp.bfloat16
LANES = 128
CHUNKS = 8
POWER = 9
VMEM_BUDGET = 56 * 1024 * 1024
GAIN_MAX = 1.8984375


def stats_kernel(
    n, ff, d_model,
    grad_ref, weight_ref, row_moment_ref, col_moment_ref, states_ref, gain_ref,
    rows_ref, cols_ref, row_factor_ref, col_factor_ref, scale_ref, normed_ref,
    grad_buf, weight_buf, row_acc, row_buf, row_recv, col_buf, col_recv, msg, all_buf,
    norm_buf, norm_got,
    load_sem, wload_sem, row_sems, col_send, col_recv_sem, msg_send, msg_recv,
    norm_send, norm_recv, pass_sems,
):
    me = lax.axis_index("fsdp")
    core = lax.axis_index("tp")
    rows, cols = grad_ref.shape
    pieces = grad_buf.shape[0]
    width = cols // pieces
    groups = width // LANES
    chunk = cols // n // LANES
    row_groups = rows // LANES

    def load(p):
        return pltpu.make_async_copy(
            grad_ref.at[:, pl.ds(pl.multiple_of(p * width, LANES), width)],
            grad_buf.at[p],
            load_sem.at[p],
        )

    for p in range(pieces):
        load(p).start()
    wload = pltpu.make_async_copy(weight_ref, weight_buf, wload_sem)
    wload.start()

    barrier = pltpu.get_barrier_semaphore()
    for d in range(1, n):
        pl.semaphore_signal(
            barrier, inc=1, device_id={"fsdp": lax.rem(me + d, n)}, device_id_type=MESH
        )
    pl.semaphore_signal(barrier, inc=1, device_id={"tp": 1 - core}, device_id_type=MESH)

    values = states_ref[...].astype(F32)
    inverse = lax.rsqrt(jnp.mean(values * values, axis=1, keepdims=True) + 1e-06)
    normed = (values * inverse * gain_ref[...].astype(F32)).astype(BF16)
    half = rows // 2
    for p in range(n):
        for h in range(2):
            at = p * rows + h * half
            norm_buf[h, p] = normed[:, at : at + half]
    pl.semaphore_wait(barrier, n)

    def send_normed(d):
        peer = lax.rem(me + d, n)
        return pltpu.make_async_remote_copy(
            src_ref=norm_buf.at[core, peer],
            dst_ref=norm_got.at[core, me],
            send_sem=norm_send.at[d],
            recv_sem=norm_recv.at[d],
            device_id={"fsdp": peer},
            device_id_type=MESH,
        )

    for d in range(1, n):
        send_normed(d).start()
    norm_got[core, me] = norm_buf[core, me]

    row_acc[...] = jnp.zeros_like(row_acc)
    step_rows = 32

    @pl.loop(0, pieces)
    def _(p):
        load(p).wait()

        def body(r, acc):
            at = pl.multiple_of(r * step_rows, step_rows)
            x = grad_buf[p, pl.ds(at, step_rows), :].astype(F32)
            sq = x * x
            lane = sq[:, :LANES]
            for g in range(1, groups):
                lane = lane + sq[:, g * LANES : (g + 1) * LANES]
            row_acc[pl.ds(at, step_rows), :] += lane
            return acc + jnp.sum(sq.reshape(step_rows // 8, 8, width), axis=0)

        acc = lax.fori_loop(0, rows // step_rows, body, jnp.zeros((8, width), F32))
        total = jnp.sum(acc, axis=0, keepdims=True)
        for g in range(groups):
            col_buf[p, g : g + 1, :] = total[:, g * LANES : (g + 1) * LANES]

    row_line = jnp.sum(jnp.transpose(row_acc[...]), axis=0, keepdims=True)
    row_buf[...] = jnp.zeros_like(row_buf)
    for g in range(row_groups):
        row_buf[g : g + 1, :] = row_line[:, g * LANES : (g + 1) * LANES]

    send_rows = pltpu.make_async_remote_copy(
        src_ref=row_buf, dst_ref=row_recv, send_sem=row_sems.at[0], recv_sem=row_sems.at[1],
        device_id={"tp": 1 - core}, device_id_type=MESH,
    )

    def send_cols(d):
        peer = lax.rem(me + d, n)
        return pltpu.make_async_remote_copy(
            src_ref=col_buf.at[peer], dst_ref=col_recv.at[d],
            send_sem=col_send.at[d], recv_sem=col_recv_sem.at[d],
            device_id={"fsdp": peer}, device_id_type=MESH,
        )

    send_rows.start()
    for d in range(1, n):
        send_cols(d).start()

    wload.wait()

    def biggest(r, m):
        x = jnp.abs(weight_buf[pl.ds(pl.multiple_of(r * 16, 16), 16), :])
        for g in range(cols // LANES):
            m = jnp.maximum(m, x[:, g * LANES : (g + 1) * LANES])
        return m

    weight_max = lax.fori_loop(0, rows // 16, biggest, jnp.zeros((16, LANES), BF16))
    weight_max = jnp.max(weight_max.astype(F32), axis=(0, 1), keepdims=True)

    send_rows.wait()
    row_total = row_buf[...] + row_recv[...]
    new_rows = 0.8 * row_moment_ref[...] + 0.2 * (row_total[:row_groups] / ff + 1e-30)
    rows_ref[...] = new_rows
    rows_summed = jnp.sum(new_rows, axis=(0, 1), keepdims=True)
    rows_least = jnp.min(new_rows, axis=(0, 1), keepdims=True)

    col_total = col_buf[me]
    for d in range(1, n):
        send_cols(d).wait()
        col_total = col_total + col_recv[d]
    msg[0:chunk] = col_total
    msg[chunk : chunk + 8] = jnp.zeros((8, LANES), F32)
    msg[chunk : chunk + 1] = jnp.broadcast_to(rows_summed, (1, LANES))
    msg[chunk + 1 : chunk + 2] = jnp.broadcast_to(rows_least, (1, LANES))
    msg[chunk + 2 : chunk + 3] = jnp.broadcast_to(weight_max, (1, LANES))

    def send_msg(d):
        return pltpu.make_async_remote_copy(
            src_ref=msg, dst_ref=all_buf.at[me],
            send_sem=msg_send.at[d], recv_sem=msg_recv.at[d],
            device_id={"fsdp": lax.rem(me + d, n)}, device_id_type=MESH,
        )

    for d in range(1, n):
        send_msg(d).start()
    all_buf[me] = msg[...]

    for d in range(1, n):
        send_normed(d).wait()
    give = pltpu.make_async_remote_copy(
        src_ref=norm_got.at[core], dst_ref=norm_got.at[core],
        send_sem=pass_sems.at[0], recv_sem=pass_sems.at[1],
        device_id={"tp": 1 - core}, device_id_type=MESH,
    )
    give.start()

    for d in range(1, n):
        send_msg(d).wait()
    summed = all_buf[0, chunk : chunk + 1, :]
    least = all_buf[0, chunk + 1 : chunk + 2, :]
    heaviest = all_buf[0, chunk + 2 : chunk + 3, :]
    for o in range(1, n):
        summed = summed + all_buf[o, chunk : chunk + 1, :]
        least = jnp.minimum(least, all_buf[o, chunk + 1 : chunk + 2, :])
        heaviest = jnp.maximum(heaviest, all_buf[o, chunk + 2 : chunk + 3, :])
    row_scale = summed / d_model
    ratio = jnp.zeros((1, LANES), F32)
    for o in range(n):
        here = slice(o * chunk, (o + 1) * chunk)
        sums = all_buf[o, 0:chunk, :]
        new_columns = 0.8 * col_moment_ref[here, :] + 0.2 * (sums / d_model + 1e-30)
        cols_ref[here, :] = new_columns
        col_factor_ref[here, :] = lax.rsqrt(new_columns)
        ratio = jnp.maximum(ratio, jnp.max(sums / new_columns, axis=0, keepdims=True))
    ratio = jnp.max(ratio, axis=1, keepdims=True)
    factor = 0.01 * jnp.sqrt(row_scale[:, 0:1]) * lax.rsqrt(new_rows)
    for g in range(row_groups):
        line = jnp.broadcast_to(factor[g : g + 1, :], (LANES, LANES))
        row_factor_ref[g * LANES : (g + 1) * LANES, :] = jnp.transpose(line)

    column_norm = d_model**0.5 * heaviest + 0.01 * jnp.sqrt(row_scale / least * ratio)
    bound = 1.02 * GAIN_MAX * d_model**0.5 * column_norm + 1e-25
    scale_ref[...] = jnp.zeros_like(scale_ref)
    scale_ref[0:1, :] = 8000.0 / bound
    scale_ref[1:2, :] = bound / 8000.0

    give.wait()
    normed_ref[...] = norm_got[...]


def statistics(n, ff, d_model, grad, weight, row_moment, col_moment, states, gain):
    rows, cols = grad.shape
    tokens = states.shape[0]
    chunk = cols // n // LANES
    half = rows // 2
    vmem = pl.BlockSpec(memory_space=pltpu.VMEM)
    hbm = pl.BlockSpec(memory_space=pl.ANY)
    shape = jax.ShapeDtypeStruct
    dma = pltpu.SemaphoreType.DMA
    return pl.pallas_call(
        functools.partial(stats_kernel, n, ff, d_model),
        out_shape=(
            shape((rows // LANES, LANES), F32),
            shape((cols // LANES, LANES), F32),
            shape((rows, LANES), F32),
            shape((cols // LANES, LANES), F32),
            shape((8, LANES), F32),
            shape((2, n, tokens, half), BF16),
        ),
        in_specs=[hbm, hbm, vmem, vmem, vmem, vmem],
        out_specs=(vmem,) * 6,
        scratch_shapes=[
            pltpu.VMEM((n, rows, cols // n), BF16),
            pltpu.VMEM((rows, cols), BF16),
            pltpu.VMEM((rows, LANES), F32),
            pltpu.VMEM((8, LANES), F32),
            pltpu.VMEM((8, LANES), F32),
            pltpu.VMEM((n, chunk, LANES), F32),
            pltpu.VMEM((n, chunk, LANES), F32),
            pltpu.VMEM((chunk + 8, LANES), F32),
            pltpu.VMEM((n, chunk + 8, LANES), F32),
            pltpu.VMEM((2, n, tokens, half), BF16),
            pltpu.VMEM((2, n, tokens, half), BF16),
            dma((n,)), dma, dma((2,)), dma((n,)), dma((n,)), dma((n,)), dma((n,)),
            dma((n,)), dma((n,)), dma((2,)),
        ],
        compiler_params=pltpu.CompilerParams(
            collective_id=0, has_side_effects=True, vmem_limit_bytes=VMEM_BUDGET
        ),
        name="statistics",
    )(
        grad, weight, row_moment.reshape(rows // LANES, LANES),
        col_moment.reshape(cols // LANES, LANES), states, gain.reshape(1, -1),
    )


def update_kernel(grad_ref, weight_ref, row_factor_ref, col_factor_ref, out_ref):
    for g in range(grad_ref.shape[1] // LANES):
        at = slice(g * LANES, (g + 1) * LANES)
        step = grad_ref[:, at].astype(F32) * row_factor_ref[...] * col_factor_ref[g : g + 1, :]
        out_ref[:, at] = (weight_ref[:, at].astype(F32) - step).astype(BF16)


def update(grad, weight, row_factor, col_factor):
    rows, cols = grad.shape
    width = 8 * LANES
    block = pl.BlockSpec((rows, width), lambda j: (0, j))
    return pl.pallas_call(
        update_kernel,
        grid=(cols // width,),
        out_shape=jax.ShapeDtypeStruct((rows, cols), BF16),
        in_specs=[
            block, block,
            pl.BlockSpec((rows, LANES), lambda j: (0, 0)),
            pl.BlockSpec((8, LANES), lambda j: (j, 0)),
        ],
        out_specs=block,
        compiler_params=pltpu.CompilerParams(vmem_limit_bytes=VMEM_BUDGET),
        name="update",
    )(grad, weight, row_factor, col_factor)


def encode(v):
    square = v * v
    fourth = square * square
    return (fourth * fourth * v).astype(BF16)


def decode(code, unscale):
    c = code.astype(F32)
    size = jnp.exp2(jnp.log2(jnp.abs(c)) * (1.0 / POWER)) * unscale
    return jnp.where(c < 0, -size, size)


def ring_kernel(
    n, weight_ref, normed_ref, gate_ref, scale_ref, out_ref,
    weight_buf, part, sent, got, load_sem, send_sem, recv_sem,
):
    steps = n // 2
    width = weight_buf.shape[2]
    tokens, half = normed_ref.shape[2], normed_ref.shape[3]
    index = lax.axis_index("fsdp")

    place = jnp.where(lax.rem(index, 2) == 0, index // 2, n - 1 - index // 2)

    def device_at(q):
        q = lax.rem(q + n, n)
        return jnp.where(q < n // 2, 2 * q, 2 * (n - 1 - q) + 1)

    neighbours = (device_at(place + 1), device_at(place - 1))

    def load(c):
        return pltpu.make_async_copy(
            weight_ref.at[:, pl.ds(pl.multiple_of(c * width, LANES), width)],
            weight_buf.at[c],
            load_sem.at[c],
        )

    for c in range(CHUNKS):
        load(c).start()

    barrier = pltpu.get_barrier_semaphore()
    for other in neighbours:
        pl.semaphore_signal(barrier, inc=1, device_id={"fsdp": other}, device_id_type=MESH)
    pl.semaphore_wait(barrier, 2)

    scale = scale_ref[0:1, 0:1]
    unscale = scale_ref[1:2, 0:1]

    def copy(way, step, c):
        return pltpu.make_async_remote_copy(
            src_ref=sent.at[way, step, c],
            dst_ref=got.at[way, step, c],
            send_sem=send_sem.at[way, step, c],
            recv_sem=recv_sem.at[way, step, c],
            device_id={"fsdp": neighbours[way]},
            device_id_type=MESH,
        )

    def pass_on(way, step, c, first):
        far = steps - step
        dest = device_at(place + far) if way == 0 else device_at(place - far)
        total = part[c, dest]
        if not first:
            copy(way, step - 1, c).wait_recv()
            total = total + decode(got[way, step - 1, c], unscale)
        sent[way, step, c] = encode(total * scale)
        copy(way, step, c).start()

    @pl.loop(0, CHUNKS // 2)
    def _(pair):
        for way in range(2):
            c = 2 * pair + way
            load(c).wait()
            product = jnp.dot(
                normed_ref[0].reshape(n * tokens, half), weight_buf[c, :half, :],
                preferred_element_type=F32,
            ) + jnp.dot(
                normed_ref[1].reshape(n * tokens, half), weight_buf[c, half:, :],
                preferred_element_type=F32,
            )
            part[c] = product.reshape(n, tokens, width)
            pass_on(way, 0, c, True)

    for step in range(1, steps):

        @pl.loop(0, CHUNKS // 2)
        def _(pair):
            for parity in range(2):
                for way in range(2):
                    pass_on(way, step, 2 * pair + parity, step == 1 and parity != way)

    @pl.loop(0, CHUNKS)
    def _(c):
        total = part[c, index]
        for way in range(2):
            copy(way, steps - 1, c).wait_recv()
            total = total + decode(got[way, steps - 1, c], unscale)
        up_values = total.astype(BF16).astype(F32)
        at = pl.ds(pl.multiple_of(c * width, LANES), width)
        gate = gate_ref[:, at].astype(F32)
        out_ref[:, at] = (gate / (1.0 + jnp.exp(-gate)) * up_values).astype(BF16)

    @pl.loop(0, CHUNKS // 2)
    def _(pair):
        for way in range(2):
            copy(way, 0, 2 * pair + way).wait_send()
            for step in range(1, steps):
                for parity in range(2):
                    copy(way, step, 2 * pair + parity).wait_send()


def project(n, weight, normed, gate, scale):
    rows, cols = weight.shape
    tokens = gate.shape[0]
    width = cols // CHUNKS
    vmem = pl.BlockSpec(memory_space=pltpu.VMEM)
    dma = pltpu.SemaphoreType.DMA
    slots = (2, n // 2, CHUNKS)
    return pl.pallas_call(
        functools.partial(ring_kernel, n),
        out_shape=jax.ShapeDtypeStruct(gate.shape, BF16),
        in_specs=[pl.BlockSpec(memory_space=pl.ANY), vmem, vmem, vmem],
        out_specs=vmem,
        scratch_shapes=[
            pltpu.VMEM((CHUNKS, rows, width), BF16),
            pltpu.VMEM((CHUNKS, n, tokens, width), F32),
            pltpu.VMEM((*slots, tokens, width), BF16),
            pltpu.VMEM((*slots, tokens, width), BF16),
            dma((CHUNKS,)), dma(slots), dma(slots),
        ],
        compiler_params=pltpu.CompilerParams(
            collective_id=1, has_side_effects=True, vmem_limit_bytes=VMEM_BUDGET
        ),
        name="project",
    )(weight, normed, gate, scale)


def kernels_fit(n, tp, rows, cols, tokens):
    ring = rows * cols * 2 + n * tokens * cols * (4 + 2 + 2) + 2 * tokens * cols * 2
    first = 2 * rows * cols * 2 + 4 * n * tokens * rows * 2 + 8 * tokens * n * rows * 4
    return (
        tp == 2
        and n >= 4
        and n % 2 == 0
        and rows % (2 * LANES) == 0
        and rows // LANES <= 8
        and cols % (8 * LANES * n) == 0
        and cols % (LANES * CHUNKS) == 0
        and tokens % 16 == 0
        and max(ring, first) <= VMEM_BUDGET - (8 << 20)
    )


def with_kernels(n, ff, d_model, weight, grad, row_moment, col_moment, states, gain, gate):
    new_rows, new_columns, row_factor, col_factor, scale, normed = statistics(
        n, ff, d_model, grad, weight, row_moment, col_moment, states, gain
    )
    new_weight = update(grad, weight, row_factor, col_factor)
    hidden = project(n, new_weight, normed, gate, scale)
    return new_weight, new_rows.reshape(-1), new_columns.reshape(-1), hidden


def with_collectives(ff, d_model, weight, grad, row_moment, col_moment, states, gain, gate):
    gradient = grad.astype(F32)
    squares = gradient * gradient + 1e-30
    row_total = lax.psum(jnp.sum(squares, axis=1), "tp")
    new_rows = 0.8 * row_moment + 0.2 * (row_total / ff)
    col_total, rows_summed = lax.psum((jnp.sum(squares, axis=0), jnp.sum(new_rows)), "fsdp")
    new_columns = 0.8 * col_moment + 0.2 * (col_total / d_model)
    row_scale = rows_summed / d_model
    change = gradient / jnp.sqrt(new_rows[:, None] * new_columns[None, :] / row_scale)
    new_weight = (weight.astype(F32) - 0.01 * change).astype(BF16)
    values = states.astype(F32)
    normed = (
        values
        * lax.rsqrt(jnp.mean(values * values, axis=1, keepdims=True) + 1e-06)
        * gain.astype(F32)
    ).astype(BF16)
    column_block = lax.all_to_all(new_weight, "fsdp", split_axis=1, concat_axis=0, tiled=True)
    up_block = jnp.dot(
        lax.all_gather(normed, "fsdp", axis=0, tiled=True),
        column_block,
        preferred_element_type=F32,
    ).astype(BF16)
    up_values = lax.all_to_all(up_block, "fsdp", split_axis=0, concat_axis=1, tiled=True)
    hidden = (jax.nn.silu(gate.astype(F32)) * up_values.astype(F32)).astype(BF16)
    return new_weight, new_rows, new_columns, hidden


def solution(mesh):
    n, tp = mesh.shape["fsdp"], mesh.shape["tp"]

    def on_device(weight, grad, row_moment, col_moment, states, gain, gate):
        rows, cols = weight.shape
        ff, d_model = cols * tp, rows * n
        arrays = (weight, grad, row_moment, col_moment, states, gain, gate)
        if kernels_fit(n, tp, rows, cols, states.shape[0]):
            return with_kernels(n, ff, d_model, *arrays)
        return with_collectives(ff, d_model, *arrays)

    return jax.shard_map(
        on_device,
        mesh=mesh,
        in_specs=(
            P(("job", "fsdp"), "tp"),
            P(("job", "fsdp"), "tp"),
            P(("job", "fsdp")),
            P(("job", "tp")),
            P(("job", "fsdp"), None),
            P("job"),
            P(("job", "fsdp"), "tp"),
        ),
        out_specs=(
            P(("job", "fsdp"), "tp"),
            P(("job", "fsdp")),
            P(("job", "tp")),
            P(("job", "fsdp"), "tp"),
        ),
        check_vma=False,
    )
```

time: 366 us -> 104 us (0.28)
  waiting for transfers between devices: 222 us -> 0 us
  Pallas kernels: 0 us -> 97.9 us
  local copies, waits for them, and re-layouts: 47.4 us -> 4.58 us
  blocking collectives: 42.7 us -> 0 us
  other arithmetic: 21 us -> 0 us
  between operations: 14.8 us -> 0.66 us
  starting transfers between devices: 8.72 us -> 0 us
  matrix products: 8.63 us -> 0 us
    all_to_all x2 -> x0, waiting for transfers between devices: 222 us -> none  [the longest x1 213 us: on_device(): lax.all_to_all(new_weight, 'fsdp', split_axis=1, concat_axis=0, tiled=True)]
    pallas_call x0 -> x3, Pallas kernels: none -> 97.9 us  [the longest x1 65 us: project(): pl.pallas_call(functools.partial(ring_kernel, n), out_shape=jax.ShapeDtyp...]
    psum x2 -> x0, blocking collectives: 42.7 us -> none  [the longest x1 40.2 us: on_device(): col_total, rows_summed = lax.psum((col_partial, jnp.sum(new_rows)), 'fsdp')]
    unnamed x17 -> x7, local copies, waits for them, and re-layouts: 35.9 us -> 3.27 us
    convert_element_type x4 -> x0, other arithmetic: 13.3 us -> none  [the longest x1 11 us: on_device(): (weight.astype(jnp.float32) - 0.01 * update).astype(jnp.bfloat16)]
    all_to_all x1 -> x0, local copies, waits for them, and re-layouts: 11.4 us -> none  [on_device(): lax.all_to_all(new_weight, 'fsdp', split_axis=1, concat_axis=0, tiled=True)]
    all_to_all x2 -> x0, starting transfers between devices: 8.68 us -> none  [the longest x1 5.11 us: on_device(): lax.all_to_all(new_weight, 'fsdp', split_axis=1, concat_axis=0, tiled=True)]
    dot_general x1 -> x0, matrix products: 8.63 us -> none  [on_device(): jnp.dot(lax.all_gather(normed, 'fsdp', axis=0, tiled=True), column_block,...]
  transfers between devices with their start and end apart: 3 -> 0, of which waited for: 2 -> 0; matrix products, arithmetic and copies ran while one was open for 7% -> 0% of each run, Pallas kernels for 0% -> 0%
where the time goes in v1:
time: 104 us; the launch traced here: 103 us
  Pallas kernels  97.9 us (94%)
  local copies, waits for them, and re-layouts  4.58 us (4%)
    pallas_call x1, Pallas kernels, project(): pl.pallas_call(functools.partial(ring_kernel, n), out_shape=jax.ShapeDtyp...  65 us
    pallas_call x1, Pallas kernels, statistics(): pl.pallas_call(functools.partial(stats_kernel, n, ff, d_model), out_shape...  20.3 us
    pallas_call x1, Pallas kernels, update(): pl.pallas_call(update_kernel, grid=(cols // width,), out_shape=jax.ShapeD...  12.6 us
    unnamed x7, local copies, waits for them, and re-layouts  3.27 us

profile of v1, /device:TPU:0, one launch (start us, length us, event | category | flops | bytes accessed | tf_op | source)
XLA Modules:
  0.0 103.2 jit_solution(14846840360133430459)
XLA Ops:
  0.6 1.3 %reshape.25.gain_ref = bf16[1,4096]{1,0:T(2,128)(2,1)} reshape(bf16[4096]{0:T(1024)(128)(2,1)} %param.12) | data formatting | bytes 16384 | tf_op jit(solution)/shard_map/reshape | solution.py:249
  1.9 20.3 %statistics.1 = (f32[4,128]{1,0:T(4,128)}, f32[64,128]{1,0:T(8,128)}, f32[512,128]{1,0:T(8,128)}, f32[64,128]{1,0:T(8,128)}, f32[8,128]{1,0:T(8,128)}, /*index=5*/bf16[2,8,48,256]{3,2,1,0:T(8,128)(2,1)}) custom-call(bf16[512,8192]{1,0:T(8,128)(2,1)} %grad_ref.3, bf16[512,8192]{1,0:T(8,128)(2,1)} %weight_ref.3, f32[4,128]{1,0:T(4,128)} %bitcast.7, ...), custom_call_target="tpu_custom_call" | custom-call | tf_op jit(solution)/shard_map/statistics/pallas_call | solution.py:216
  22.3 12.6 %update.1.weight_ref = bf16[512,8192]{1,0:T(8,128)(2,1)} custom-call(bf16[512,8192]{1,0:T(8,128)(2,1)} %grad_ref.3, bf16[512,8192]{1,0:T(8,128)(2,1)} %weight_ref.3, f32[512,128]{1,0:T(8,128)} %get-tuple-element.10.row_factor_ref, f32[64,128]{1,0:T(8,128)} %get-tuple-element.11.col_factor_ref), custom_call_target="tpu_custom_call" | custom-call | tf_op jit(solution)/shard_map/update/pallas_call | solution.py:264
  34.9 0.0 copy-start.1
  34.9 0.0 copy-start
  34.9 65.0 %project.1 = bf16[48,8192]{1,0:T(8,128)(2,1)} custom-call(bf16[512,8192]{1,0:T(8,128)(2,1)} %update.1.weight_ref, bf16[2,8,48,256]{3,2,1,0:T(8,128)(2,1)} %get-tuple-element.14.normed_ref, bf16[48,8192]{1,0:T(8,128)(2,1)} %gate_ref.1, f32[8,128]{1,0:T(8,128)} %get-tuple-element.15.scale_ref), custom_call_target="tpu_custom_call" | custom-call | tf_op jit(solution)/shard_map/project/pallas_call | solution.py:396
  99.9 0.0 copy-done.1
  99.9 0.6 copy.14
  100.5 0.0 copy-done
  100.5 0.6 copy.15
  101.1 2.1 %copy.16 = bf16[48,8192]{1,0:T(8,128)(2,1)} copy(bf16[48,8192]{1,0:T(8,128)(2,1)} %project.1) | data formatting | bytes 1572864
Async XLA Ops:
  34.9 65.0 %copy-start.1 = (f32[4,128]{1,0:T(4,128)S(1)}, f32[4,128]{1,0:T(4,128)}, u32[]{:S(2)}) copy-start(f32[4,128]{1,0:T(4,128)} %get-tuple-element.12) | copy-start | bytes 6148
  34.9 65.6 %copy-start = (f32[64,128]{1,0:T(8,128)S(1)}, f32[64,128]{1,0:T(8,128)}, u32[]{:S(2)}) copy-start(f32[64,128]{1,0:T(8,128)} %get-tuple-element.13) | copy-start | bytes 98308

commit v2 on v1

v2 whole, which is shorter than its diff:
```python
import functools
import jax
import jax.numpy as jnp
from jax import lax
from jax.experimental import pallas as pl
from jax.experimental.pallas import tpu as pltpu
from jax.sharding import PartitionSpec as P

MESH = pl.DeviceIdType.MESH
F32 = jnp.float32
BF16 = jnp.bfloat16
LANES = 128
CHUNKS = 8
POWER = 9
VMEM_BUDGET = 56 * 1024 * 1024
GAIN_MAX = 1.8984375


def encode(v):
    square = v * v
    fourth = square * square
    return (fourth * fourth * v).astype(BF16)


def decode(code, unscale):
    c = code.astype(F32)
    size = jnp.exp2(jnp.log2(jnp.abs(c)) * (1.0 / POWER)) * unscale
    return jnp.where(c < 0, -size, size)


def step_kernel(
    n, ff, d_model,
    grad_ref, weight_ref, row_moment_ref, col_moment_ref, states_ref, gain_ref,
    new_weight_ref, rows_ref, cols_ref, up_ref,
    grad_buf, weight_buf, row_acc, row_buf, row_recv, col_buf, col_recv, msg, all_buf,
    norm_buf, norm_got, row_factor, col_factor, part, sent, got,
    load_sem, wload_sem, store_sem, row_sems, col_send, col_recv_sem, msg_send, msg_recv,
    norm_send, norm_recv, pass_sems, send_sem, recv_sem,
):
    me = lax.axis_index("fsdp")
    core = lax.axis_index("tp")
    rows, cols = grad_ref.shape
    width = cols // CHUNKS
    groups = width // LANES
    chunk = cols // n // LANES
    row_groups = rows // LANES
    tokens = states_ref.shape[0]
    half = rows // 2
    steps = n // 2

    def columns(c):
        return pl.ds(pl.multiple_of(c * width, LANES), width)

    def load(c):
        return pltpu.make_async_copy(grad_ref.at[:, columns(c)], grad_buf.at[c], load_sem.at[c])

    def wload(c):
        return pltpu.make_async_copy(
            weight_ref.at[:, columns(c)], weight_buf.at[c], wload_sem.at[c]
        )

    def store(c):
        return pltpu.make_async_copy(
            weight_buf.at[c], new_weight_ref.at[:, columns(c)], store_sem.at[c]
        )

    for c in range(CHUNKS):
        load(c).start()
    for c in range(CHUNKS):
        wload(c).start()

    barrier = pltpu.get_barrier_semaphore()
    for d in range(1, n):
        pl.semaphore_signal(
            barrier, inc=1, device_id={"fsdp": lax.rem(me + d, n)}, device_id_type=MESH
        )
    pl.semaphore_signal(barrier, inc=1, device_id={"tp": 1 - core}, device_id_type=MESH)

    values = states_ref[...].astype(F32)
    inverse = lax.rsqrt(jnp.mean(values * values, axis=1, keepdims=True) + 1e-06)
    normed = (values * inverse * gain_ref[...].astype(F32)).astype(BF16)
    for p in range(n):
        for h in range(2):
            at = p * rows + h * half
            norm_buf[h, p] = normed[:, at : at + half]
    pl.semaphore_wait(barrier, n)

    def send_normed(d):
        peer = lax.rem(me + d, n)
        return pltpu.make_async_remote_copy(
            src_ref=norm_buf.at[core, peer],
            dst_ref=norm_got.at[core, me],
            send_sem=norm_send.at[d],
            recv_sem=norm_recv.at[d],
            device_id={"fsdp": peer},
            device_id_type=MESH,
        )

    for d in range(1, n):
        send_normed(d).start()
    norm_got[core, me] = norm_buf[core, me]

    row_acc[...] = jnp.zeros_like(row_acc)
    step_rows = 32

    @pl.loop(0, CHUNKS)
    def _(c):
        load(c).wait()

        def body(r, acc):
            at = pl.multiple_of(r * step_rows, step_rows)
            x = grad_buf[c, pl.ds(at, step_rows), :].astype(F32)
            sq = x * x
            lane = sq[:, :LANES]
            for g in range(1, groups):
                lane = lane + sq[:, g * LANES : (g + 1) * LANES]
            row_acc[pl.ds(at, step_rows), :] += lane
            return acc + jnp.sum(sq.reshape(step_rows // 8, 8, width), axis=0)

        acc = lax.fori_loop(
            0, rows // step_rows, body, jnp.zeros((8, width), F32), unroll=4
        )
        total = jnp.sum(acc, axis=0, keepdims=True)
        for g in range(groups):
            col_buf[c, g : g + 1, :] = total[:, g * LANES : (g + 1) * LANES]

    def send_cols(d):
        peer = lax.rem(me + d, n)
        return pltpu.make_async_remote_copy(
            src_ref=col_buf.at[peer], dst_ref=col_recv.at[d],
            send_sem=col_send.at[d], recv_sem=col_recv_sem.at[d],
            device_id={"fsdp": peer}, device_id_type=MESH,
        )

    for d in range(1, n):
        send_cols(d).start()

    row_line = jnp.sum(jnp.transpose(row_acc[...]), axis=0, keepdims=True)
    row_buf[...] = jnp.zeros_like(row_buf)
    for g in range(row_groups):
        row_buf[g : g + 1, :] = row_line[:, g * LANES : (g + 1) * LANES]
    send_rows = pltpu.make_async_remote_copy(
        src_ref=row_buf, dst_ref=row_recv, send_sem=row_sems.at[0], recv_sem=row_sems.at[1],
        device_id={"tp": 1 - core}, device_id_type=MESH,
    )
    send_rows.start()

    def biggest(c, m):
        wload(c).wait()

        def inner(r, m):
            x = jnp.abs(weight_buf[c, pl.ds(pl.multiple_of(r * 64, 64), 64), :])
            for g in range(groups):
                for k in range(4):
                    m = jnp.maximum(m, x[k * 16 : k * 16 + 16, g * LANES : (g + 1) * LANES])
            return m

        return lax.fori_loop(0, rows // 64, inner, m)

    weight_max = lax.fori_loop(0, CHUNKS, biggest, jnp.zeros((16, LANES), BF16))
    weight_max = jnp.max(weight_max.astype(F32), axis=(0, 1), keepdims=True)

    send_rows.wait()
    row_total = row_buf[...] + row_recv[...]
    new_rows = 0.8 * row_moment_ref[...] + 0.2 * (row_total[:row_groups] / ff + 1e-30)
    rows_ref[...] = new_rows
    rows_summed = jnp.sum(new_rows, axis=(0, 1), keepdims=True)
    rows_least = jnp.min(new_rows, axis=(0, 1), keepdims=True)

    col_total = col_buf[me]
    for d in range(1, n):
        send_cols(d).wait()
        col_total = col_total + col_recv[d]
    msg[0:chunk] = col_total
    msg[chunk : chunk + 8] = jnp.zeros((8, LANES), F32)
    msg[chunk : chunk + 1] = jnp.broadcast_to(rows_summed, (1, LANES))
    msg[chunk + 1 : chunk + 2] = jnp.broadcast_to(rows_least, (1, LANES))
    msg[chunk + 2 : chunk + 3] = jnp.broadcast_to(weight_max, (1, LANES))

    def send_msg(d):
        return pltpu.make_async_remote_copy(
            src_ref=msg, dst_ref=all_buf.at[me],
            send_sem=msg_send.at[d], recv_sem=msg_recv.at[d],
            device_id={"fsdp": lax.rem(me + d, n)}, device_id_type=MESH,
        )

    for d in range(1, n):
        send_msg(d).start()
    all_buf[me] = msg[...]

    for d in range(1, n):
        send_normed(d).wait()
    give = pltpu.make_async_remote_copy(
        src_ref=norm_got.at[core], dst_ref=norm_got.at[core],
        send_sem=pass_sems.at[0], recv_sem=pass_sems.at[1],
        device_id={"tp": 1 - core}, device_id_type=MESH,
    )
    give.start()
    factor = 0.01 * lax.rsqrt(new_rows)
    for g in range(row_groups):
        line = jnp.broadcast_to(factor[g : g + 1, :], (LANES, LANES))
        row_factor[g * LANES : (g + 1) * LANES, :] = jnp.transpose(line)

    for d in range(1, n):
        send_msg(d).wait()
    summed = all_buf[0, chunk : chunk + 1, :]
    least = all_buf[0, chunk + 1 : chunk + 2, :]
    heaviest = all_buf[0, chunk + 2 : chunk + 3, :]
    for o in range(1, n):
        summed = summed + all_buf[o, chunk : chunk + 1, :]
        least = jnp.minimum(least, all_buf[o, chunk + 1 : chunk + 2, :])
        heaviest = jnp.maximum(heaviest, all_buf[o, chunk + 2 : chunk + 3, :])
    row_scale = summed / d_model
    root = jnp.sqrt(row_scale)
    ratio = jnp.zeros((1, LANES), F32)
    for o in range(n):
        here = slice(o * chunk, (o + 1) * chunk)
        sums = all_buf[o, 0:chunk, :]
        new_columns = 0.8 * col_moment_ref[here, :] + 0.2 * (sums / d_model + 1e-30)
        cols_ref[here, :] = new_columns
        scaled = lax.rsqrt(new_columns) * root
        col_factor[o] = scaled
        ratio = jnp.maximum(ratio, jnp.max(sums / new_columns, axis=0, keepdims=True))
    ratio = jnp.max(ratio, axis=1, keepdims=True)

    column_norm = d_model**0.5 * heaviest + 0.01 * jnp.sqrt(row_scale / least * ratio)
    bound = (1.02 * GAIN_MAX * d_model**0.5 * column_norm + 1e-25)[:, 0:1]
    scale = 8000.0 / bound
    unscale = bound / 8000.0
    give.wait()

    place = jnp.where(lax.rem(me, 2) == 0, me // 2, n - 1 - me // 2)

    def device_at(q):
        q = lax.rem(q + n, n)
        return jnp.where(q < n // 2, 2 * q, 2 * (n - 1 - q) + 1)

    neighbours = (device_at(place + 1), device_at(place - 1))

    def copy(way, step, c):
        return pltpu.make_async_remote_copy(
            src_ref=sent.at[way, step, c],
            dst_ref=got.at[way, step, c],
            send_sem=send_sem.at[way, step, c],
            recv_sem=recv_sem.at[way, step, c],
            device_id={"fsdp": neighbours[way]},
            device_id_type=MESH,
        )

    def pass_on(way, step, c, first):
        far = steps - step
        dest = device_at(place + far) if way == 0 else device_at(place - far)
        total = part[c, dest]
        if not first:
            copy(way, step - 1, c).wait_recv()
            total = total + decode(got[way, step - 1, c], unscale)
        sent[way, step, c] = encode(total * scale)
        copy(way, step, c).start()

    @pl.loop(0, CHUNKS // 2)
    def _(pair):
        for way in range(2):
            c = 2 * pair + way

            @pl.loop(0, row_groups)
            def _(r):
                block = pl.ds(pl.multiple_of(r * LANES, LANES), LANES)
                for g in range(groups):
                    at = slice(g * LANES, (g + 1) * LANES)
                    change = (
                        grad_buf[c, block, at].astype(F32)
                        * row_factor[block, :]
                        * col_factor[c, g : g + 1, :]
                    )
                    weight_buf[c, block, at] = (
                        weight_buf[c, block, at].astype(F32) - change
                    ).astype(BF16)

            store(c).start()
            product = jnp.dot(
                norm_got[0].reshape(n * tokens, half), weight_buf[c, :half, :],
                preferred_element_type=F32,
            ) + jnp.dot(
                norm_got[1].reshape(n * tokens, half), weight_buf[c, half:, :],
                preferred_element_type=F32,
            )
            part[c] = product.reshape(n, tokens, width)
            pass_on(way, 0, c, True)
            pass_on(1 - way, 1, c, True)

    @pl.loop(0, CHUNKS // 2)
    def _(pair):
        for way in range(2):
            pass_on(way, 1, 2 * pair + way, False)

    for step in range(2, steps):

        @pl.loop(0, CHUNKS)
        def _(c):
            for way in range(2):
                pass_on(way, step, c, False)

    @pl.loop(0, CHUNKS)
    def _(c):
        total = part[c, me]
        for way in range(2):
            copy(way, steps - 1, c).wait_recv()
            total = total + decode(got[way, steps - 1, c], unscale)
        up_ref[:, columns(c)] = total.astype(BF16)

    @pl.loop(0, CHUNKS // 2)
    def _(pair):
        for way in range(2):
            store(2 * pair + way).wait()
            copy(way, 0, 2 * pair + way).wait_send()
            for step in range(1, steps):
                for parity in range(2):
                    copy(way, step, 2 * pair + parity).wait_send()


def kernels_fit(n, tp, rows, cols, tokens):
    held = 2 * rows * cols * 2 + n * tokens * cols * (4 + 2 + 2) + tokens * cols * 2
    held += 4 * n * tokens * rows * 2 + 2 * tokens * n * rows * 4
    return (
        tp == 2
        and n >= 4
        and n == CHUNKS
        and rows % (2 * LANES) == 0
        and rows // LANES <= 8
        and cols % (8 * LANES * n) == 0
        and tokens % 16 == 0
        and held <= VMEM_BUDGET - (4 << 20)
    )


def with_kernels(n, ff, d_model, weight, grad, row_moment, col_moment, states, gain, gate):
    rows, cols = grad.shape
    tokens = states.shape[0]
    chunk = cols // n // LANES
    half = rows // 2
    width = cols // CHUNKS
    slots = (2, n // 2, CHUNKS)
    vmem = pl.BlockSpec(memory_space=pltpu.VMEM)
    hbm = pl.BlockSpec(memory_space=pl.ANY)
    shape = jax.ShapeDtypeStruct
    dma = pltpu.SemaphoreType.DMA
    new_weight, new_rows, new_columns, up_values = pl.pallas_call(
        functools.partial(step_kernel, n, ff, d_model),
        out_shape=(
            shape((rows, cols), BF16),
            shape((rows // LANES, LANES), F32),
            shape((cols // LANES, LANES), F32),
            shape((tokens, cols), BF16),
        ),
        in_specs=[hbm, hbm, vmem, vmem, vmem, vmem],
        out_specs=(hbm, vmem, vmem, vmem),
        scratch_shapes=[
            pltpu.VMEM((CHUNKS, rows, width), BF16),
            pltpu.VMEM((CHUNKS, rows, width), BF16),
            pltpu.VMEM((rows, LANES), F32),
            pltpu.VMEM((8, LANES), F32),
            pltpu.VMEM((8, LANES), F32),
            pltpu.VMEM((n, chunk, LANES), F32),
            pltpu.VMEM((n, chunk, LANES), F32),
            pltpu.VMEM((chunk + 8, LANES), F32),
            pltpu.VMEM((n, chunk + 8, LANES), F32),
            pltpu.VMEM((2, n, tokens, half), BF16),
            pltpu.VMEM((2, n, tokens, half), BF16),
            pltpu.VMEM((rows, LANES), F32),
            pltpu.VMEM((CHUNKS, width // LANES, LANES), F32),
            pltpu.VMEM((CHUNKS, n, tokens, width), F32),
            pltpu.VMEM((*slots, tokens, width), BF16),
            pltpu.VMEM((*slots, tokens, width), BF16),
            dma((CHUNKS,)), dma((CHUNKS,)), dma((CHUNKS,)), dma((2,)), dma((n,)), dma((n,)),
            dma((n,)), dma((n,)), dma((n,)), dma((n,)), dma((2,)), dma(slots), dma(slots),
        ],
        compiler_params=pltpu.CompilerParams(
            collective_id=0, has_side_effects=True, vmem_limit_bytes=VMEM_BUDGET
        ),
        name="whole_step",
    )(
        grad, weight, row_moment.reshape(rows // LANES, LANES),
        col_moment.reshape(cols // LANES, LANES), states, gain.reshape(1, -1),
    )
    hidden = (jax.nn.silu(gate.astype(F32)) * up_values.astype(F32)).astype(BF16)
    return new_weight, new_rows.reshape(-1), new_columns.reshape(-1), hidden


def with_collectives(ff, d_model, weight, grad, row_moment, col_moment, states, gain, gate):
    gradient = grad.astype(F32)
    squares = gradient * gradient + 1e-30
    row_total = lax.psum(jnp.sum(squares, axis=1), "tp")
    new_rows = 0.8 * row_moment + 0.2 * (row_total / ff)
    col_total, rows_summed = lax.psum((jnp.sum(squares, axis=0), jnp.sum(new_rows)), "fsdp")
    new_columns = 0.8 * col_moment + 0.2 * (col_total / d_model)
    row_scale = rows_summed / d_model
    change = gradient / jnp.sqrt(new_rows[:, None] * new_columns[None, :] / row_scale)
    new_weight = (weight.astype(F32) - 0.01 * change).astype(BF16)
    values = states.astype(F32)
    normed = (
        values
        * lax.rsqrt(jnp.mean(values * values, axis=1, keepdims=True) + 1e-06)
        * gain.astype(F32)
    ).astype(BF16)
    column_block = lax.all_to_all(new_weight, "fsdp", split_axis=1, concat_axis=0, tiled=True)
    up_block = jnp.dot(
        lax.all_gather(normed, "fsdp", axis=0, tiled=True),
        column_block,
        preferred_element_type=F32,
    ).astype(BF16)
    up_values = lax.all_to_all(up_block, "fsdp", split_axis=0, concat_axis=1, tiled=True)
    hidden = (jax.nn.silu(gate.astype(F32)) * up_values.astype(F32)).astype(BF16)
    return new_weight, new_rows, new_columns, hidden


def solution(mesh):
    n, tp = mesh.shape["fsdp"], mesh.shape["tp"]

    def on_device(weight, grad, row_moment, col_moment, states, gain, gate):
        rows, cols = weight.shape
        ff, d_model = cols * tp, rows * n
        arrays = (weight, grad, row_moment, col_moment, states, gain, gate)
        if kernels_fit(n, tp, rows, cols, states.shape[0]):
            return with_kernels(n, ff, d_model, *arrays)
        return with_collectives(ff, d_model, *arrays)

    return jax.shard_map(
        on_device,
        mesh=mesh,
        in_specs=(
            P(("job", "fsdp"), "tp"),
            P(("job", "fsdp"), "tp"),
            P(("job", "fsdp")),
            P(("job", "tp")),
            P(("job", "fsdp"), None),
            P("job"),
            P(("job", "fsdp"), "tp"),
        ),
        out_specs=(
            P(("job", "fsdp"), "tp"),
            P(("job", "fsdp")),
            P(("job", "tp")),
            P(("job", "fsdp"), "tp"),
        ),
        check_vma=False,
    )
```

time: 104 us -> 95.2 us (0.915)
  Pallas kernels: 97.9 us -> 81.6 us
  local copies, waits for them, and re-layouts: 4.58 us -> 10.3 us
  other arithmetic: 0 us -> 2.46 us
    pallas_call x3 -> x1, Pallas kernels: 97.9 us -> 81.6 us  [with_kernels(): pl.pallas_call(functools.partial(step_kernel, n, ff, d_model), out_shape=...]
    unnamed x7 -> x9, local copies, waits for them, and re-layouts: 3.27 us -> 8.99 us
    convert_element_type x0 -> x1, other arithmetic: none -> 2.46 us  [with_kernels(): (jax.nn.silu(gate.astype(F32)) * up_values.astype(F32)).astype(BF16)]
where the time goes in v2:
time: 95.2 us; the launch traced here: 95 us
  Pallas kernels  81.6 us (86%)
  local copies, waits for them, and re-layouts  10.3 us (11%)
  other arithmetic  2.46 us (3%)
    pallas_call x1, Pallas kernels, with_kernels(): pl.pallas_call(functools.partial(step_kernel, n, ff, d_model), out_shape=...  81.6 us
    unnamed x9, local copies, waits for them, and re-layouts  8.99 us
    convert_element_type x1, other arithmetic, with_kernels(): (jax.nn.silu(gate.astype(F32)) * up_values.astype(F32)).astype(BF16)  2.46 us

profile of v2, /device:TPU:0, one launch (start us, length us, event | category | flops | bytes accessed | tf_op | source)
XLA Modules:
  0.0 95.0 jit_solution(1030904665066237968)
XLA Ops:
  0.6 1.3 %reshape.25.gain_ref = bf16[1,4096]{1,0:T(2,128)(2,1)} reshape(bf16[4096]{0:T(1024)(128)(2,1)} %param.12) | data formatting | bytes 16384 | tf_op jit(solution)/shard_map/reshape | solution.py:383
  1.9 0.0 copy-start
  1.9 81.6 %whole_step.1 = (bf16[512,8192]{1,0:T(8,128)(2,1)}, f32[4,128]{1,0:T(4,128)}, f32[64,128]{1,0:T(8,128)}, bf16[48,8192]{1,0:T(8,128)(2,1)}) custom-call(bf16[512,8192]{1,0:T(8,128)(2,1)} %grad_ref.1, bf16[512,8192]{1,0:T(8,128)(2,1)} %weight_ref.1, f32[4,128]{1,0:T(4,128)} %bitcast.7, f32[64,128]{1,0:T(8,128)} %bitcast.4, bf16[48,4096]{1,0:T(8,128)(2,1)} %states_ref.1, ...), custom_call_target="tpu_custom_call" | custom-call | tf_op jit(solution)/shard_map/whole_step/pallas_call | solution.py:347
  83.6 0.0 copy-done
  83.6 2.5 %fusion.4 = bf16[48,8192]{1,0:T(8,128)(2,1)} fusion(bf16[48,8192]{1,0:T(8,128)(2,1)} %get-tuple-element.11, bf16[48,8192]{1,0:T(8,128)(2,1)S(1)} %copy-done), kind=kLoop, calls=%fused_computation.6 | loop fusion | flops 3145728 | bytes 2359296 | tf_op jit(solution)/shard_map/convert_element_type | solution.py:385
  86.0 0.0 copy-start.2
  86.0 0.0 copy-start.1
  86.0 7.8 %copy.14 = bf16[512,8192]{1,0:T(8,128)(2,1)} copy(bf16[512,8192]{1,0:T(8,128)(2,1)} %get-tuple-element.16) | data formatting | bytes 16777216
  93.8 0.0 copy-done.2
  93.8 0.6 copy.15
  94.4 0.0 copy-done.1
  94.4 0.6 copy.16
Async XLA Ops:
  1.9 81.6 %copy-start = (bf16[48,8192]{1,0:T(8,128)(2,1)S(1)}, bf16[48,8192]{1,0:T(8,128)(2,1)}, u32[]{:S(2)}) copy-start(bf16[48,8192]{1,0:T(8,128)(2,1)} %param.13) | copy-start | bytes 2359300
  86.0 7.8 %copy-start.2 = (f32[4,128]{1,0:T(4,128)S(1)}, f32[4,128]{1,0:T(4,128)}, u32[]{:S(2)}) copy-start(f32[4,128]{1,0:T(4,128)} %get-tuple-element.9) | copy-start | bytes 6148
  86.0 8.4 %copy-start.1 = (f32[64,128]{1,0:T(8,128)S(1)}, f32[64,128]{1,0:T(8,128)}, u32[]{:S(2)}) copy-start(f32[64,128]{1,0:T(8,128)} %get-tuple-element.10) | copy-start | bytes 98308

commit v3 on v2

--- a/solution.py
+++ b/solution.py
@@ -10,7 +10,7 @@
 F32 = jnp.float32
 BF16 = jnp.bfloat16
 LANES = 128
-CHUNKS = 8
+HALVES = 2
 POWER = 9
 VMEM_BUDGET = 56 * 1024 * 1024
 GAIN_MAX = 1.8984375
@@ -40,7 +40,8 @@
     me = lax.axis_index("fsdp")
     core = lax.axis_index("tp")
     rows, cols = grad_ref.shape
-    width = cols // CHUNKS
+    chunks = HALVES * n
+    width = cols // chunks
     groups = width // LANES
     chunk = cols // n // LANES
     row_groups = rows // LANES
@@ -64,9 +65,9 @@
             weight_buf.at[c], new_weight_ref.at[:, columns(c)], store_sem.at[c]
         )
 
-    for c in range(CHUNKS):
+    for c in range(chunks):
         load(c).start()
-    for c in range(CHUNKS):
+    for c in range(chunks):
         wload(c).start()
 
     barrier = pltpu.get_barrier_semaphore()
@@ -78,11 +79,13 @@
 
     values = states_ref[...].astype(F32)
     inverse = lax.rsqrt(jnp.mean(values * values, axis=1, keepdims=True) + 1e-06)
-    normed = (values * inverse * gain_ref[...].astype(F32)).astype(BF16)
-    for p in range(n):
-        for h in range(2):
-            at = p * rows + h * half
-            norm_buf[h, p] = normed[:, at : at + half]
+    gain = gain_ref[...].astype(F32)
+    for g in range(d_model // LANES):
+        at = g * LANES
+        p, h, inside = at // rows, at % rows // half, at % half
+        norm_buf[h, p, :, inside : inside + LANES] = (
+            values[:, at : at + LANES] * inverse * gain[g : g + 1, :]
+        ).astype(BF16)
     pl.semaphore_wait(barrier, n)
 
     def send_normed(d):
@@ -103,26 +106,32 @@
     row_acc[...] = jnp.zeros_like(row_acc)
     step_rows = 32
 
-    @pl.loop(0, CHUNKS)
-    def _(c):
-        load(c).wait()
-
-        def body(r, acc):
+    @pl.loop(0, n)
+    def _(p):
+        for k in range(HALVES):
+            load(HALVES * p + k).wait()
+
+        def body(r, accs):
             at = pl.multiple_of(r * step_rows, step_rows)
-            x = grad_buf[c, pl.ds(at, step_rows), :].astype(F32)
-            sq = x * x
-            lane = sq[:, :LANES]
-            for g in range(1, groups):
-                lane = lane + sq[:, g * LANES : (g + 1) * LANES]
-            row_acc[pl.ds(at, step_rows), :] += lane
-            return acc + jnp.sum(sq.reshape(step_rows // 8, 8, width), axis=0)
-
-        acc = lax.fori_loop(
-            0, rows // step_rows, body, jnp.zeros((8, width), F32), unroll=4
-        )
-        total = jnp.sum(acc, axis=0, keepdims=True)
-        for g in range(groups):
-            col_buf[c, g : g + 1, :] = total[:, g * LANES : (g + 1) * LANES]
+            lane = row_acc[pl.ds(at, step_rows), :]
+            out = []
+            for k in range(HALVES):
+                x = grad_buf[HALVES * p + k, pl.ds(at, step_rows), :].astype(F32)
+                sq = x * x
+                for g in range(groups):
+                    lane = lane + sq[:, g * LANES : (g + 1) * LANES]
+                out.append(accs[k] + jnp.sum(sq.reshape(step_rows // 8, 8, width), axis=0))
+            row_acc[pl.ds(at, step_rows), :] = lane
+            return tuple(out)
+
+        accs = lax.fori_loop(
+            0, rows // step_rows, body, (jnp.zeros((8, width), F32),) * HALVES, unroll=4
+        )
+        for k in range(HALVES):
+            total = jnp.sum(accs[k], axis=0, keepdims=True)
+            for g in range(groups):
+                line = k * groups + g
+                col_buf[p, line : line + 1, :] = total[:, g * LANES : (g + 1) * LANES]
 
     def send_cols(d):
         peer = lax.rem(me + d, n)
@@ -157,7 +166,7 @@
 
         return lax.fori_loop(0, rows // 64, inner, m)
 
-    weight_max = lax.fori_loop(0, CHUNKS, biggest, jnp.zeros((16, LANES), BF16))
+    weight_max = lax.fori_loop(0, chunks, biggest, jnp.zeros((16, LANES), BF16))
     weight_max = jnp.max(weight_max.astype(F32), axis=(0, 1), keepdims=True)
 
     send_rows.wait()
@@ -257,7 +266,7 @@
         sent[way, step, c] = encode(total * scale)
         copy(way, step, c).start()
 
-    @pl.loop(0, CHUNKS // 2)
+    @pl.loop(0, n)
     def _(pair):
         for way in range(2):
             c = 2 * pair + way
@@ -270,7 +279,7 @@
                     change = (
                         grad_buf[c, block, at].astype(F32)
                         * row_factor[block, :]
-                        * col_factor[c, g : g + 1, :]
+                        * col_factor[pair, way * groups + g : way * groups + g + 1, :]
                     )
                     weight_buf[c, block, at] = (
                         weight_buf[c, block, at].astype(F32) - change
@@ -288,19 +297,19 @@
             pass_on(way, 0, c, True)
             pass_on(1 - way, 1, c, True)
 
-    @pl.loop(0, CHUNKS // 2)
+    @pl.loop(0, n)
     def _(pair):
         for way in range(2):
             pass_on(way, 1, 2 * pair + way, False)
 
     for step in range(2, steps):
 
-        @pl.loop(0, CHUNKS)
+        @pl.loop(0, chunks)
         def _(c):
             for way in range(2):
                 pass_on(way, step, c, False)
 
-    @pl.loop(0, CHUNKS)
+    @pl.loop(0, chunks)
     def _(c):
         total = part[c, me]
         for way in range(2):
@@ -308,7 +317,7 @@
             total = total + decode(got[way, steps - 1, c], unscale)
         up_ref[:, columns(c)] = total.astype(BF16)
 
-    @pl.loop(0, CHUNKS // 2)
+    @pl.loop(0, n)
     def _(pair):
         for way in range(2):
             store(2 * pair + way).wait()
@@ -318,16 +327,71 @@
                     copy(way, step, 2 * pair + parity).wait_send()
 
 
+def finish_kernel(
+    made_ref, gate_ref, up_ref, rows_in, cols_in, weight_ref, hidden_ref, rows_out, cols_out,
+    buf, in_sem, out_sem,
+):
+    pieces, height = buf.shape[0], buf.shape[1]
+
+    def fetch(p):
+        at = pl.ds(p * height, height)
+        return pltpu.make_async_copy(made_ref.at[at, :], buf.at[p], in_sem.at[p])
+
+    def store(p):
+        at = pl.ds(p * height, height)
+        return pltpu.make_async_copy(buf.at[p], weight_ref.at[at, :], out_sem.at[p])
+
+    for p in range(pieces):
+        fetch(p).start()
+    rows_out[...] = rows_in[...]
+    cols_out[...] = cols_in[...]
+    each = gate_ref.shape[1] // pieces
+    for p in range(pieces):
+        at = slice(p * each, (p + 1) * each)
+        gate = gate_ref[:, at].astype(F32)
+        silu = gate / (1.0 + jnp.exp(-gate))
+        hidden_ref[:, at] = (silu * up_ref[:, at].astype(F32)).astype(BF16)
+        fetch(p).wait()
+        store(p).start()
+    for p in range(pieces):
+        store(p).wait()
+
+
+def finish(made, gate, up_values, new_rows, new_columns):
+    rows, cols = made.shape
+    pieces = 16
+    vmem = pl.BlockSpec(memory_space=pltpu.VMEM)
+    hbm = pl.BlockSpec(memory_space=pl.ANY)
+    return pl.pallas_call(
+        finish_kernel,
+        out_shape=(
+            jax.ShapeDtypeStruct(made.shape, BF16),
+            jax.ShapeDtypeStruct(gate.shape, BF16),
+            jax.ShapeDtypeStruct(new_rows.shape, F32),
+            jax.ShapeDtypeStruct(new_columns.shape, F32),
+        ),
+        in_specs=[hbm, vmem, vmem, vmem, vmem],
+        out_specs=(hbm, vmem, vmem, vmem),
+        scratch_shapes=[
+            pltpu.VMEM((pieces, rows // pieces, cols), BF16),
+            pltpu.SemaphoreType.DMA((pieces,)),
+            pltpu.SemaphoreType.DMA((pieces,)),
+        ],
+        compiler_params=pltpu.CompilerParams(vmem_limit_bytes=VMEM_BUDGET),
+        name="finish",
+    )(made, gate, up_values, new_rows, new_columns)
+
+
 def kernels_fit(n, tp, rows, cols, tokens):
     held = 2 * rows * cols * 2 + n * tokens * cols * (4 + 2 + 2) + tokens * cols * 2
     held += 4 * n * tokens * rows * 2 + 2 * tokens * n * rows * 4
     return (
         tp == 2
         and n >= 4
-        and n == CHUNKS
         and rows % (2 * LANES) == 0
         and rows // LANES <= 8
         and cols % (8 * LANES * n) == 0
+        and cols % (HALVES * LANES * n) == 0
         and tokens % 16 == 0
         and held <= VMEM_BUDGET - (4 << 20)
     )
@@ -338,8 +402,9 @@
     tokens = states.shape[0]
     chunk = cols // n // LANES
     half = rows // 2
-    width = cols // CHUNKS
-    slots = (2, n // 2, CHUNKS)
+    chunks = HALVES * n
+    width = cols // chunks
+    slots = (2, n // 2, chunks)
     vmem = pl.BlockSpec(memory_space=pltpu.VMEM)
     hbm = pl.BlockSpec(memory_space=pl.ANY)
     shape = jax.ShapeDtypeStruct
@@ -355,8 +420,8 @@
         in_specs=[hbm, hbm, vmem, vmem, vmem, vmem],
         out_specs=(hbm, vmem, vmem, vmem),
         scratch_shapes=[
-            pltpu.VMEM((CHUNKS, rows, width), BF16),
-            pltpu.VMEM((CHUNKS, rows, width), BF16),
+            pltpu.VMEM((chunks, rows, width), BF16),
+            pltpu.VMEM((chunks, rows, width), BF16),
             pltpu.VMEM((rows, LANES), F32),
             pltpu.VMEM((8, LANES), F32),
             pltpu.VMEM((8, LANES), F32),
@@ -367,11 +432,11 @@
             pltpu.VMEM((2, n, tokens, half), BF16),
             pltpu.VMEM((2, n, tokens, half), BF16),
             pltpu.VMEM((rows, LANES), F32),
-            pltpu.VMEM((CHUNKS, width // LANES, LANES), F32),
-            pltpu.VMEM((CHUNKS, n, tokens, width), F32),
+            pltpu.VMEM((n, chunk, LANES), F32),
+            pltpu.VMEM((chunks, n, tokens, width), F32),
             pltpu.VMEM((*slots, tokens, width), BF16),
             pltpu.VMEM((*slots, tokens, width), BF16),
-            dma((CHUNKS,)), dma((CHUNKS,)), dma((CHUNKS,)), dma((2,)), dma((n,)), dma((n,)),
+            dma((chunks,)), dma((chunks,)), dma((chunks,)), dma((2,)), dma((n,)), dma((n,)),
             dma((n,)), dma((n,)), dma((n,)), dma((n,)), dma((2,)), dma(slots), dma(slots),
         ],
         compiler_params=pltpu.CompilerParams(
@@ -380,9 +445,11 @@
         name="whole_step",
     )(
         grad, weight, row_moment.reshape(rows // LANES, LANES),
-        col_moment.reshape(cols // LANES, LANES), states, gain.reshape(1, -1),
+        col_moment.reshape(cols // LANES, LANES), states, gain.reshape(-1, LANES),
     )
-    hidden = (jax.nn.silu(gate.astype(F32)) * up_values.astype(F32)).astype(BF16)
+    new_weight, hidden, new_rows, new_columns = finish(
+        new_weight, gate, up_values, new_rows, new_columns
+    )
     return new_weight, new_rows.reshape(-1), new_columns.reshape(-1), hidden
 
 

time: 95.2 us -> 92.4 us (0.971)
  local copies, waits for them, and re-layouts: 10.3 us -> 0 us
  Pallas kernels: 81.6 us -> 91.6 us
  other arithmetic: 2.46 us -> 0 us
    unnamed x9 -> x0, local copies, waits for them, and re-layouts: 8.99 us -> none
    pallas_call x0 -> x1, Pallas kernels: none -> 8.83 us  [finish(): pl.pallas_call(finish_kernel, out_shape=(jax.ShapeDtypeStruct(made.shape,...]
    convert_element_type x1 -> x0, other arithmetic: 2.46 us -> none  [with_kernels(): (jax.nn.silu(gate.astype(F32)) * up_values.astype(F32)).astype(BF16)]
    reshape x1 -> x0, local copies, waits for them, and re-layouts: 1.31 us -> none  [with_kernels(): gain.reshape(1, -1)]
    pallas_call x1, Pallas kernels: 81.6 us -> 82.8 us  [with_kernels(): pl.pallas_call(functools.partial(step_kernel, n, ff, d_model), out_shape=...]
where the time goes in v3:
time: 92.4 us; the launch traced here: 92.2 us
  Pallas kernels  91.6 us (99%)
    pallas_call x1, Pallas kernels, with_kernels(): pl.pallas_call(functools.partial(step_kernel, n, ff, d_model), out_shape=...  82.8 us
    pallas_call x1, Pallas kernels, finish(): pl.pallas_call(finish_kernel, out_shape=(jax.ShapeDtypeStruct(made.shape,...  8.83 us

profile of v3, /device:TPU:0, one launch (start us, length us, event | category | flops | bytes accessed | tf_op | source)
XLA Modules:
  0.0 92.2 jit_solution(3156809789297954182)
XLA Ops:
  0.6 82.8 %whole_step.1 = (bf16[512,8192]{1,0:T(8,128)(2,1)}, f32[4,128]{1,0:T(4,128)}, f32[64,128]{1,0:T(8,128)}, bf16[48,8192]{1,0:T(8,128)(2,1)}) custom-call(bf16[512,8192]{1,0:T(8,128)(2,1)} %grad_ref.1, bf16[512,8192]{1,0:T(8,128)(2,1)} %weight_ref.1, f32[4,128]{1,0:T(4,128)} %bitcast.7, f32[64,128]{1,0:T(8,128)} %bitcast.5, bf16[48,4096]{1,0:T(8,128)(2,1)} %states_ref.1, ...), custom_call_target="tpu_custom_call" | custom-call | tf_op jit(solution)/shard_map/whole_step/pallas_call | solution.py:412
  83.4 8.8 %finish.1 = (bf16[512,8192]{1,0:T(8,128)(2,1)}, bf16[48,8192]{1,0:T(8,128)(2,1)}, f32[4,128]{1,0:T(4,128)}, f32[64,128]{1,0:T(8,128)}) custom-call(bf16[512,8192]{1,0:T(8,128)(2,1)} %get-tuple-element.12.made_ref, bf16[48,8192]{1,0:T(8,128)(2,1)} %gate_ref.1, bf16[48,8192]{1,0:T(8,128)(2,1)} %get-tuple-element.13.up_ref, ...), custom_call_target="tpu_custom_call" | custom-call | tf_op jit(solution)/shard_map/finish/pallas_call | solution.py:365

commit v4 on v3

--- a/solution.py
+++ b/solution.py
@@ -329,20 +329,17 @@
 
 def finish_kernel(
     made_ref, gate_ref, up_ref, rows_in, cols_in, weight_ref, hidden_ref, rows_out, cols_out,
-    buf, in_sem, out_sem,
+    out_sem,
 ):
-    pieces, height = buf.shape[0], buf.shape[1]
-
-    def fetch(p):
-        at = pl.ds(p * height, height)
-        return pltpu.make_async_copy(made_ref.at[at, :], buf.at[p], in_sem.at[p])
+    pieces = out_sem.shape[0]
+    height = made_ref.shape[0] // pieces
 
     def store(p):
         at = pl.ds(p * height, height)
-        return pltpu.make_async_copy(buf.at[p], weight_ref.at[at, :], out_sem.at[p])
+        return pltpu.make_async_copy(made_ref.at[at, :], weight_ref.at[at, :], out_sem.at[p])
 
     for p in range(pieces):
-        fetch(p).start()
+        store(p).start()
     rows_out[...] = rows_in[...]
     cols_out[...] = cols_in[...]
     each = gate_ref.shape[1] // pieces
@@ -351,8 +348,6 @@
         gate = gate_ref[:, at].astype(F32)
         silu = gate / (1.0 + jnp.exp(-gate))
         hidden_ref[:, at] = (silu * up_ref[:, at].astype(F32)).astype(BF16)
-        fetch(p).wait()
-        store(p).start()
     for p in range(pieces):
         store(p).wait()
 
@@ -373,11 +368,9 @@
         in_specs=[hbm, vmem, vmem, vmem, vmem],
         out_specs=(hbm, vmem, vmem, vmem),
         scratch_shapes=[
-            pltpu.VMEM((pieces, rows // pieces, cols), BF16),
-            pltpu.SemaphoreType.DMA((pieces,)),
             pltpu.SemaphoreType.DMA((pieces,)),
         ],
-        compiler_params=pltpu.CompilerParams(vmem_limit_bytes=VMEM_BUDGET),
+        compiler_params=pltpu.CompilerParams(vmem_limit_bytes=16 * 1024 * 1024),
         name="finish",
     )(made, gate, up_values, new_rows, new_columns)
 
@@ -412,7 +405,7 @@
     new_weight, new_rows, new_columns, up_values = pl.pallas_call(
         functools.partial(step_kernel, n, ff, d_model),
         out_shape=(
-            shape((rows, cols), BF16),
+            pltpu.VMEM((rows, cols), BF16),
             shape((rows // LANES, LANES), F32),
             shape((cols // LANES, LANES), F32),
             shape((tokens, cols), BF16),
@@ -440,7 +433,7 @@
             dma((n,)), dma((n,)), dma((n,)), dma((n,)), dma((2,)), dma(slots), dma(slots),
         ],
         compiler_params=pltpu.CompilerParams(
-            collective_id=0, has_side_effects=True, vmem_limit_bytes=VMEM_BUDGET
+            collective_id=0, has_side_effects=True, vmem_limit_bytes=48 * 1024 * 1024
         ),
         name="whole_step",
     )(

time: 92.4 us -> 90.9 us (0.984)
  Pallas kernels: 91.6 us -> 87.4 us
  local copies, waits for them, and re-layouts: 0 us -> 2.56 us
    pallas_call x1, Pallas kernels: 8.83 us -> 4.3 us  [finish(): pl.pallas_call(finish_kernel, out_shape=(jax.ShapeDtypeStruct(made.shape,...]
    unnamed x0 -> x8, local copies, waits for them, and re-layouts: none -> 2.56 us
where the time goes in v4:
time: 90.9 us; the launch traced here: 90.6 us
  Pallas kernels  87.4 us (96%)
  local copies, waits for them, and re-layouts  2.56 us (3%)
    pallas_call x1, Pallas kernels, with_kernels(): pl.pallas_call(functools.partial(step_kernel, n, ff, d_model), out_shape=...  83.1 us
    pallas_call x1, Pallas kernels, finish(): pl.pallas_call(finish_kernel, out_shape=(jax.ShapeDtypeStruct(made.shape,...  4.3 us
    unnamed x8, local copies, waits for them, and re-layouts  2.56 us

profile of v4, /device:TPU:0, one launch (start us, length us, event | category | flops | bytes accessed | tf_op | source)
XLA Modules:
  0.0 90.6 jit_solution(18171509892682059398)
XLA Ops:
  0.6 0.0 copy-start
  0.6 83.1 %whole_step.1 = (bf16[512,8192]{1,0:T(8,128)(2,1)S(1)}, f32[4,128]{1,0:T(4,128)}, f32[64,128]{1,0:T(8,128)}, bf16[48,8192]{1,0:T(8,128)(2,1)}) custom-call(bf16[512,8192]{1,0:T(8,128)(2,1)} %grad_ref.1, bf16[512,8192]{1,0:T(8,128)(2,1)} %weight_ref.1, f32[4,128]{1,0:T(4,128)} %bitcast.7, f32[64,128]{1,0:T(8,128)} %bitcast.5, bf16[48,4096]{1,0:T(8,128)(2,1)} %states_ref.1, ...), custom_call_target="tpu_custom_call" | custom-call | tf_op jit(solution)/shard_map/whole_step/pallas_call | solution.py:405
  83.7 0.0 copy-done
  83.7 0.0 copy-start.1
  83.7 1.1 %copy-done.1 = bf16[48,8192]{1,0:T(8,128)(2,1)S(1)} copy-done((bf16[48,8192]{1,0:T(8,128)(2,1)S(1)}, bf16[48,8192]{1,0:T(8,128)(2,1)}, u32[]{:S(2)}) %copy-start.1) | copy-done | bytes 786456
  84.9 0.0 copy-start.2
  84.9 0.8 copy-done.2
  85.6 0.0 copy-start.3
  85.6 0.7 copy-done.3
  86.3 4.3 %finish.1 = (bf16[512,8192]{1,0:T(8,128)(2,1)}, bf16[48,8192]{1,0:T(8,128)(2,1)}, f32[4,128]{1,0:T(4,128)}, f32[64,128]{1,0:T(8,128)}) custom-call(bf16[512,8192]{1,0:T(8,128)(2,1)S(1)} %get-tuple-element.12.made_ref, bf16[48,8192]{1,0:T(8,128)(2,1)S(1)} %copy-done, bf16[48,8192]{1,0:T(8,128)(2,1)S(1)} %copy-done.1, f32[4,128]{1,0:T(4,128)S(1)} %copy-done.3, ...), custom_call_target="tpu_custom_call" | custom-call | tf_op jit(solution)/shard_map/finish/pallas_call | solution.py:360
Async XLA Ops:
  0.6 83.1 %copy-start = (bf16[48,8192]{1,0:T(8,128)(2,1)S(1)}, bf16[48,8192]{1,0:T(8,128)(2,1)}, u32[]{:S(2)}) copy-start(bf16[48,8192]{1,0:T(8,128)(2,1)} %gate_ref.1) | copy-start | bytes 2359300
  83.7 1.1 %copy-start.1 = (bf16[48,8192]{1,0:T(8,128)(2,1)S(1)}, bf16[48,8192]{1,0:T(8,128)(2,1)}, u32[]{:S(2)}) copy-start(bf16[48,8192]{1,0:T(8,128)(2,1)} %get-tuple-element.13.up_ref) | copy-start | bytes 2359300
  84.9 0.8 copy-start.2
  85.6 0.7 copy-start.3
